TPU v7x, 512 devices: a whole 4x8x8 slice. The times are simulated.
512 devices in a mesh: tm: 128 (over z_lo, x, y, core), series: 4 (over z_hi).
Axes of the slice: x: 4, y: 8, z: 8 (z_hi: 4, z_lo: 2; z = z_hi * 2 + z_lo), core: 2. Of those that a mesh axis runs over, the one named last changes fastest.
Arguments:
- time_query: bfloat16 [20, 8192, 512], P('series', 'tm'), may hold values from -160 to 160
- time_key: bfloat16 [20, 8192, 512], P('series', 'tm'), may hold values from -6 to 6
- time_value: bfloat16 [20, 8192, 512], P('series', 'tm'), may hold values from -6 to 6
- group_query: bfloat16 [20, 8192, 512], P('series', 'tm'), may hold values from -160 to 160
- group_key: bfloat16 [20, 8192, 512], P('series', 'tm'), may hold values from -6 to 6
- group_value: bfloat16 [20, 8192, 512], P('series', 'tm'), may hold values from -6 to 6
- out_time: bfloat16 [512, 768], P('series'), may hold values from -0.25 to 0.25
- out_group: bfloat16 [512, 768], P('series'), may hold values from -0.25 to 0.25
- series_group: int32 [20], replicated, may hold values from 0 to 1, as said below
- band_width: int32 [8], replicated, may hold values from 2 to 16, as said below
- cotangent: bfloat16 [20, 8192, 768], P('series', 'tm'), may hold values from -6 to 6
Outputs:
- grad_time_query: bfloat16 [20, 8192, 512], P('series', 'tm')
- grad_time_key: bfloat16 [20, 8192, 512], P('series', 'tm')
- grad_time_value: bfloat16 [20, 8192, 512], P('series', 'tm')
- grad_group_query: bfloat16 [20, 8192, 512], P('series', 'tm')
- grad_group_key: bfloat16 [20, 8192, 512], P('series', 'tm')
- grad_group_value: bfloat16 [20, 8192, 512], P('series', 'tm')
- grad_out_time: float32 [512, 768], P('series', 'tm')
- grad_out_group: float32 [512, 768], P('series', 'tm')
Inputs may be any that keep to these rules, and one draw needn't show every extreme that they name: `series_group`: series with equal numbers form one group; there are two groups, one of exactly 16 series and one of exactly 4. `band_width`: some head's band is exactly 16.
All inputs are finite; a program needn't handle non-finite values.
Results may differ from a plain program's by a relative error of at most 0.0058.
Values may be sent and summed in bfloat16 or wider, within the bound.
No kernel may reach another device: no remote copies, remote signals or barrier semaphores. Data moves between devices by JAX's collectives and lax.ppermute only.
A program may use at most 128 MiB of HBM per device.

v0:
```python
import jax
import jax.numpy as jnp
from jax import lax
from jax.sharding import PartitionSpec as P

HEAD_DIM = 64
BAND = 16


masked_score = -1e30


def passed_along(value, axis, steps):
    count = lax.axis_size(axis)
    leading, last = (max(0, -steps), min(count, count - steps))
    return lax.ppermute(value, axis, [(source, source + steps) for source in range(leading, last)])


def soft_weights(scores, keep_mask):
    scores = jnp.where(keep_mask, scores, masked_score)
    row_top = jnp.max(scores, axis=-1, keepdims=True)
    weights = jnp.exp(scores - row_top)
    return weights / jnp.sum(weights, axis=-1, keepdims=True)


def score_grad(probabilities, grad_prob, score_scale):
    grad_inner = lax.optimization_barrier(grad_prob.astype(jnp.bfloat16)).astype(jnp.float32)
    centred = grad_inner - jnp.sum(grad_inner * probabilities, axis=-1, keepdims=True)
    return probabilities * centred * score_scale


def temporal_attend(query_rows, key_ext, value_ext, out_grad, band_width, first_row):
    ser_count, block_rows, row_width = query_rows.shape
    head_count = band_width.shape[0]
    head_depth = row_width // head_count
    border_rows = key_ext.shape[1] - block_rows
    score_scale = head_depth ** (-0.5)
    query_heads = query_rows.reshape(ser_count, block_rows, head_count, head_depth)
    key_heads = key_ext.reshape(ser_count, block_rows + border_rows, head_count, head_depth)
    value_heads = value_ext.reshape(ser_count, block_rows + border_rows, head_count, head_depth)
    grad_heads = out_grad.reshape(ser_count, block_rows, head_count, head_depth)
    scores = (
        jnp.einsum("sthd,sihd->shti", query_heads, key_heads, preferred_element_type=jnp.float32)
        * score_scale
    )
    query_pos = lax.broadcasted_iota(jnp.int32, (block_rows, block_rows + border_rows), 0)
    key_pos = lax.broadcasted_iota(jnp.int32, (block_rows, block_rows + border_rows), 1)
    offset = query_pos + border_rows - key_pos
    absolute = first_row + key_pos - border_rows
    in_band = (
        (offset[None] >= 0) & (offset[None] < band_width[:, None, None]) & (absolute[None] >= 0)
    )
    probabilities = soft_weights(scores, in_band[None])
    rounded = probabilities.astype(jnp.bfloat16)
    mixed_out = jnp.einsum(
        "shti,sihd->sthd", rounded, value_heads, preferred_element_type=jnp.float32
    )
    grad_value = jnp.einsum(
        "shti,sthd->sihd", rounded, grad_heads, preferred_element_type=jnp.float32
    )
    grad_prob = jnp.einsum(
        "sthd,sihd->shti", grad_heads, value_heads, preferred_element_type=jnp.float32
    )
    grad_score = score_grad(probabilities, grad_prob, score_scale)
    grad_query = jnp.einsum(
        "shti,sihd->sthd",
        grad_score,
        key_heads.astype(jnp.float32),
        precision=lax.Precision.HIGHEST,
    )
    grad_key = jnp.einsum(
        "shti,sthd->sihd",
        grad_score,
        query_heads.astype(jnp.float32),
        precision=lax.Precision.HIGHEST,
    )
    ext_rows = block_rows + border_rows
    return (
        mixed_out.reshape(ser_count, block_rows, row_width),
        grad_query.reshape(ser_count, block_rows, row_width),
        grad_key.reshape(ser_count, ext_rows, row_width),
        grad_value.reshape(ser_count, ext_rows, row_width),
    )


def group_attend(query_rows, key_rows, value_rows, out_grad, series_group):
    ser_count, block_rows, row_width = query_rows.shape
    head_count = row_width // HEAD_DIM
    score_scale = HEAD_DIM ** (-0.5)
    query_heads = query_rows.reshape(ser_count, block_rows, head_count, HEAD_DIM)
    key_heads = key_rows.reshape(ser_count, block_rows, head_count, HEAD_DIM)
    value_heads = value_rows.reshape(ser_count, block_rows, head_count, HEAD_DIM)
    grad_heads = out_grad.reshape(ser_count, block_rows, head_count, HEAD_DIM)
    scores = (
        jnp.einsum("sthd,rthd->thsr", query_heads, key_heads, preferred_element_type=jnp.float32)
        * score_scale
    )
    same_group = series_group[:, None] == series_group[None, :]
    probabilities = soft_weights(scores, same_group[None, None])
    rounded = probabilities.astype(jnp.bfloat16)
    mixed_out = jnp.einsum(
        "thsr,rthd->sthd", rounded, value_heads, preferred_element_type=jnp.float32
    )
    grad_value = jnp.einsum(
        "thsr,sthd->rthd", rounded, grad_heads, preferred_element_type=jnp.float32
    )
    grad_prob = jnp.einsum(
        "sthd,rthd->thsr", grad_heads, value_heads, preferred_element_type=jnp.float32
    )
    grad_score = score_grad(probabilities, grad_prob, score_scale)
    grad_query = jnp.einsum(
        "thsr,rthd->sthd",
        grad_score,
        key_heads.astype(jnp.float32),
        precision=lax.Precision.HIGHEST,
    )
    grad_key = jnp.einsum(
        "thsr,sthd->rthd",
        grad_score,
        query_heads.astype(jnp.float32),
        precision=lax.Precision.HIGHEST,
    )
    out_shape = (ser_count, block_rows, row_width)
    return (
        mixed_out.reshape(out_shape),
        grad_query.reshape(out_shape),
        grad_key.reshape(out_shape),
        grad_value.reshape(out_shape),
    )


def group_local(moved_parts, series_group):
    query_rows, key_rows, value_rows, out_grad = moved_parts
    mixed_out, grad_query, grad_key, grad_value = group_attend(
        query_rows, key_rows, value_rows, out_grad, series_group
    )
    return (
        mixed_out.astype(jnp.bfloat16),
        grad_query.astype(jnp.bfloat16),
        grad_key.astype(jnp.bfloat16),
        grad_value.astype(jnp.bfloat16),
    )


def per_device(
    time_query,
    time_key,
    time_value,
    group_query,
    group_key,
    group_value,
    out_time,
    out_group,
    series_group,
    band_width,
    cotangent,
):
    ser_dev, block_rows, row_width = time_query.shape
    border_rows = BAND - 1
    w_time, w_group = (
        lax.all_gather(out_time, "series", axis=0, tiled=True),
        lax.all_gather(out_group, "series", axis=0, tiled=True),
    )
    cot_flat = cotangent.reshape(-1, cotangent.shape[2])

    def back_project(weight):
        product = lax.dot_general(
            cot_flat, weight, (((1,), (1,)), ((), ())), preferred_element_type=jnp.float32
        )
        return product.astype(jnp.bfloat16).reshape(ser_dev, block_rows, row_width)

    d_time = back_project(w_time)
    d_group = back_project(w_group)
    rim_key, rim_value = passed_along(
        (time_key[:, block_rows - border_rows :], time_value[:, block_rows - border_rows :]),
        "tm",
        1,
    )
    key_ext = jnp.concatenate([rim_key, time_key], axis=1)
    value_ext = jnp.concatenate([rim_value, time_value], axis=1)
    first_row = lax.axis_index("tm") * block_rows
    temporal_mixture, temporal_query_gradient, extended_key_gradient, extended_value_gradient = (
        temporal_attend(time_query, key_ext, value_ext, d_time, band_width, first_row)
    )
    time_out = temporal_mixture.astype(jnp.bfloat16)
    pulled_key_rows, pulled_value_rows = passed_along(
        (extended_key_gradient[:, :border_rows], extended_value_gradient[:, :border_rows]), "tm", -1
    )
    empty_padding_rows = jnp.zeros((ser_dev, block_rows - border_rows, row_width), jnp.float32)
    grad_tk = (
        extended_key_gradient[:, border_rows:]
        + jnp.concatenate([empty_padding_rows, pulled_key_rows], axis=1)
    ).astype(jnp.bfloat16)
    temporal_value_gradient = (
        extended_value_gradient[:, border_rows:]
        + jnp.concatenate([empty_padding_rows, pulled_value_rows], axis=1)
    ).astype(jnp.bfloat16)
    temporal_query_gradient = temporal_query_gradient.astype(jnp.bfloat16)
    moved_parts = (
        lax.all_to_all(group_query, "series", split_axis=1, concat_axis=0, tiled=True),
        lax.all_to_all(group_key, "series", split_axis=1, concat_axis=0, tiled=True),
        lax.all_to_all(group_value, "series", split_axis=1, concat_axis=0, tiled=True),
        lax.all_to_all(d_group, "series", split_axis=1, concat_axis=0, tiled=True),
    )
    results = group_local(moved_parts, series_group)
    group_out, grad_gq, grad_gk, grad_gv = (
        lax.all_to_all(results[0], "series", split_axis=0, concat_axis=1, tiled=True),
        lax.all_to_all(results[1], "series", split_axis=0, concat_axis=1, tiled=True),
        lax.all_to_all(results[2], "series", split_axis=0, concat_axis=1, tiled=True),
        lax.all_to_all(results[3], "series", split_axis=0, concat_axis=1, tiled=True),
    )
    grad_scale = (ser_dev * block_rows * lax.axis_size("series") * lax.axis_size("tm")) ** (-0.5)
    term_time = (
        lax.dot_general(
            time_out.reshape(-1, row_width),
            cot_flat,
            (((0,), (0,)), ((), ())),
            preferred_element_type=jnp.float32,
        )
        * grad_scale
    )
    term_group = (
        lax.dot_general(
            group_out.reshape(-1, row_width),
            cot_flat,
            (((0,), (0,)), ((), ())),
            preferred_element_type=jnp.float32,
        )
        * grad_scale
    )
    partial_sums = (
        lax.psum_scatter(term_time, "tm", scatter_dimension=1, tiled=True),
        lax.psum_scatter(term_group, "tm", scatter_dimension=1, tiled=True),
    )
    grad_wt, grad_wg = (
        lax.psum_scatter(partial_sums[0], "series", scatter_dimension=0, tiled=True),
        lax.psum_scatter(partial_sums[1], "series", scatter_dimension=0, tiled=True),
    )
    return (
        temporal_query_gradient,
        grad_tk,
        temporal_value_gradient,
        grad_gq,
        grad_gk,
        grad_gv,
        grad_wt,
        grad_wg,
    )


def solution(mesh):
    placed = (
        P("series", "tm", None),
        P("series", "tm", None),
        P("series", "tm", None),
        P("series", "tm", None),
        P("series", "tm", None),
        P("series", "tm", None),
        P("series", None),
        P("series", None),
        P(),
        P(),
        P("series", "tm", None),
    )
    return jax.shard_map(
        per_device,
        mesh=mesh,
        in_specs=placed,
        out_specs=(
            P("series", "tm", None),
            P("series", "tm", None),
            P("series", "tm", None),
            P("series", "tm", None),
            P("series", "tm", None),
            P("series", "tm", None),
            P("series", "tm"),
            P("series", "tm"),
        ),
        check_vma=False,
    )
```

profile of v0, /device:TPU:1, one launch (start us, length us, event | category | flops | bytes accessed | tf_op | source)
XLA Modules:
  0.0 798.8 jit_solution(5145301826097418971)
XLA Ops:
  8.2 4.6 collective-permute-start
  13.7 17.4 %collective-permute-start.1 = (bf16[5,15,512]{2,1,0:T(8,128)(2,1)S(1)}, bf16[5,15,512]{2,1,0:T(8,128)(2,1)S(1)}, u32[]{:S(2)}, u32[]{:S(2)}) collective-permute-start(bf16[5,15,512]{2,1,0:T(8,128)(2,1)S(1)} %slice.19), channel_id=1, source_target_pairs={{0,4},{4,8},{8,12},{12,16},{16,20},{20,24},{24,28},{28,32},{32,36}... | collective-permute-start | bytes 230408 | tf_op jit(solution)/shard_map/ppermute | solution.py:16
  33.1 8.6 %all-to-all-start.3 = ((bf16[5,64,512]{2,0,1:T(8,128)(2,1)}), bf16[5,64,512]{2,0,1:T(8,128)(2,1)}, u32[]{:S(2)}, u32[]{:S(2)}) async-start(bf16[5,64,512]{2,0,1:T(8,128)(2,1)} %copy.160), calls=%async_computation.3 | async-start | bytes 1048576 | tf_op jit(solution)/shard_map/all_to_all | solution.py:202
  41.9 26.7 %all_gather.6 = bf16[512,768]{1,0:T(8,128)(2,1)S(1)} all-gather(bf16[128,768]{1,0:T(8,128)(2,1)S(1)} %copy-done.27), channel_id=1, replica_groups=mesh['tm'=128,'series'=4] {'series'}, dimensions={0}, use_global_device_ids=true | all-gather | bytes 983040 | tf_op jit(solution)/shard_map/all_gather | solution.py:161
  68.5 17.9 %all_gather.7 = bf16[512,768]{1,0:T(8,128)(2,1)S(1)} all-gather(bf16[128,768]{1,0:T(8,128)(2,1)S(1)} %copy-done.28), channel_id=1, replica_groups=mesh['tm'=128,'series'=4] {'series'}, dimensions={0}, use_global_device_ids=true | all-gather | bytes 983040 | tf_op jit(solution)/shard_map/all_gather | solution.py:162
  94.3 6.3 all-to-all-start.1
  102.1 6.9 fusion.53
  110.8 5.0 all-to-all-start
  120.4 7.7 collective-permute-start.2
  135.0 3.3 copy.156
  143.1 6.9 all-to-all-start.7
  150.0 7.3 convolution_convert_fusion.5
  157.2 3.1 bitcast_multiply_fusion
  161.8 5.1 all-to-all-start.2
  168.8 310.6 %fusion.52 = (f32[512,8]{0,1:T(8,128)S(1)}, f32[512,8]{0,1:T(8,128)S(1)}) fusion(f32[512,768]{0,1:T(8,128)} %bitcast_multiply_fusion, f32[512,768]{0,1:T(8,128)} %convolution_multiply_fusion), kind=kCustom, calls=%all-reduce-scatter.2 | all-reduce-scatter fusion | flops 1048577 | bytes 3180544
  483.3 8.8 %collective-permute-start.35 = (f32[512,6]{0,1:T(8,128)S(1)}, f32[512,6]{0,1:T(8,128)S(1)}, u32[]{:S(2)}, u32[]{:S(2)}) collective-permute-start(f32[512,6]{0,1:T(8,128)S(1)} %slice.28), channel_id=1, source_target_pairs={{0,128},{4,132},{8,136},{12,140},{16,144},{20,148},{24,152},{28,15... | collective-permute-start | bytes 36872
  500.7 20.4 %collective-permute-start.26 = (f32[512,8]{0,1:T(8,128)S(1)}, f32[512,8]{0,1:T(8,128)S(1)}, u32[]{:S(2)}, u32[]{:S(2)}) collective-permute-start(f32[512,8]{0,1:T(8,128)S(1)} %get-tuple-element.50), channel_id=1, source_target_pairs={{0,92},{4,96},{8,100},{12,104},{16,108},{20,112},{24,116},{28,120}... | collective-permute-start | bytes 49160
  528.3 3.0 collective-permute-start.20
  535.8 4.9 collective-permute-start.17
  547.0 3.1 collective-permute-start.14
  552.7 4.2 collective-permute-start.12
  557.9 4.4 collective-permute-start.11
  562.3 4.7 collective-permute-start.10
  569.0 3.4 collective-permute-start.8
  572.4 3.0 collective-permute-start.7
  575.4 14.8 %fusion.10 = f32[16,8,20,20]{3,1,2,0:T(8,128)} fusion(bf16[16,8,20,20]{3,1,2,0:T(8,128)(2,1)S(1)} %copy.214, f32[16,8,20,20]{3,1,2,0:T(8,128)S(1)} %copy-done.9, f32[16,8,20]{1,2,0:T(8,128)S(1)} %copy-done.21), kind=kOutput, calls=%fused_computation.14 | output fusion | flops 412179 | bytes 522240 | tf_op jit(solution)/shard_map/sub | solution.py:28
  592.5 4.3 collective-permute-start.6
  603.9 2.9 fusion.18
  610.1 4.7 all-to-all-start.4
  620.1 2.9 collective-permute-start.60
  623.0 4.2 convolution_convert_fusion.4
  628.9 3.5 collective-permute-start.58
  634.4 2.8 collective-permute-start.56
  642.2 6.7 all-to-all-start.5
  657.5 7.3 fusion.45
  676.1 4.0 collective-permute-start.49
  683.1 2.8 collective-permute-start.46
  685.8 3.5 collective-permute-start.45
  691.6 7.1 all-to-all-start.6
  698.7 3.8 collective-permute-start.44
  705.1 4.8 collective-permute-start.42
  712.3 3.8 collective-permute-start.40
  717.1 8.1 %concatenate.16 = f32[512,262]{0,1:T(8,128)S(1)} concatenate(f32[512,6]{0,1:T(8,128)S(1)} %copy-done.41, f32[512,8]{0,1:T(8,128)S(1)} %copy-done.35, f32[512,8]{0,1:T(8,128)S(1)} %copy-done.37, f32[512,8]{0,1:T(8,128)S(1)} %copy-done.39, f32[512,8]{0,1:T(8,128)S(1)} %copy-done.43, f32[512,8]{0,1:T(8,128)S(1)} %copy-done.45, f32[512,8]{0,1:T(8,128)S(1)} %copy-done.47, ...), dimensions={1} | concatenate | bytes 1073152
  729.2 5.5 collective-permute-start.38
  736.1 3.1 collective-permute-start.36
  740.1 9.6 %concatenate.17 = f32[512,262]{0,1:T(8,128)S(1)} concatenate(f32[512,6]{0,1:T(8,128)S(1)} %copy-done.33, f32[512,8]{0,1:T(8,128)S(1)} %copy-done.73, f32[512,8]{0,1:T(8,128)S(1)} %copy-done.75, f32[512,8]{0,1:T(8,128)S(1)} %copy-done.83, f32[512,8]{0,1:T(8,128)S(1)} %copy-done.87, f32[512,8]{0,1:T(8,128)S(1)} %copy-done.91, f32[512,8]{0,1:T(8,128)S(1)} %copy-done.93, ...), dimensions={1} | concatenate | bytes 1073152
  754.3 7.8 reduce-scatter.7.cloned.1.call-done
  762.1 29.6 %reduce-scatter.9.cloned.1.call-done = f32[128,6]{0,1:T(8,128)} async-done(((f32[512,6]{0,1:T(8,128)}), f32[128,6]{0,1:T(8,128)}) %reduce-scatter.9.cloned.1.call-update) | async-done | bytes 3088 | tf_op jit(solution)/shard_map/reduce_scatter | solution.py:237
  (400 shorter events, 136.5 us)
Async XLA Ops:
  8.2 84.3 %collective-permute-start = (bf16[5,15,512]{2,1,0:T(8,128)(2,1)S(1)}, bf16[5,15,512]{2,1,0:T(8,128)(2,1)S(1)}, u32[]{:S(2)}, u32[]{:S(2)}) collective-permute-start(bf16[5,15,512]{2,1,0:T(8,128)(2,1)S(1)} %slice.18), channel_id=1, source_target_pairs={{0,4},{4,8},{8,12},{12,16},{16,20},{20,24},{24,28},{28,32},{32,36}... | collective-permute-start | bytes 230408 | tf_op jit(solution)/shard_map/ppermute | solution.py:16
  13.7 79.2 %collective-permute-start.1 = (bf16[5,15,512]{2,1,0:T(8,128)(2,1)S(1)}, bf16[5,15,512]{2,1,0:T(8,128)(2,1)S(1)}, u32[]{:S(2)}, u32[]{:S(2)}) collective-permute-start(bf16[5,15,512]{2,1,0:T(8,128)(2,1)S(1)} %slice.19), channel_id=1, source_target_pairs={{0,4},{4,8},{8,12},{12,16},{16,20},{20,24},{24,28},{28,32},{32,36}... | collective-permute-start | bytes 230408 | tf_op jit(solution)/shard_map/ppermute | solution.py:16
  33.1 60.7 %all-to-all-start.3 = ((bf16[5,64,512]{2,0,1:T(8,128)(2,1)}), bf16[5,64,512]{2,0,1:T(8,128)(2,1)}, u32[]{:S(2)}, u32[]{:S(2)}) async-start(bf16[5,64,512]{2,0,1:T(8,128)(2,1)} %copy.160), calls=%async_computation.3 | async-start | bytes 1048576 | tf_op jit(solution)/shard_map/all_to_all | solution.py:202
  110.8 20.3 %all-to-all-start = ((bf16[5,64,512]{2,0,1:T(8,128)(2,1)}), bf16[5,64,512]{2,0,1:T(8,128)(2,1)}, u32[]{:S(2)}, u32[]{:S(2)}) async-start(bf16[5,64,512]{2,0,1:T(8,128)(2,1)} %copy.150), calls=%async_computation | async-start | bytes 1048576 | tf_op jit(solution)/shard_map/all_to_all | solution.py:200
  120.4 371.8 %collective-permute-start.2 = (f32[5,15,512]{2,1,0:T(8,128)}, f32[5,15,512]{2,1,0:T(8,128)S(1)}, u32[]{:S(2)}, u32[]{:S(2)}) collective-permute-start(f32[5,15,512]{2,1,0:T(8,128)} %copy.186), channel_id=1, source_target_pairs={{4,0},{8,4},{12,8},{16,12},{20,16},{24,20},{28,24},{32,28},{36,32}... | collective-permute-start | bytes 460808 | tf_op jit(solution)/shard_map/ppermute | solution.py:16
  143.1 18.7 %all-to-all-start.7 = ((bf16[20,16,512]{2,1,0:T(8,128)(2,1)}), bf16[20,16,512]{2,1,0:T(8,128)(2,1)S(1)}, u32[]{:S(2)}, u32[]{:S(2)}) async-start(bf16[20,16,512]{2,1,0:T(8,128)(2,1)} %convert_element_type.115), calls=%async_computation.8 | async-start | bytes 655360 | tf_op jit(solution)/shard_map/all_to_all | solution.py:207
  161.8 380.8 %all-to-all-start.2 = ((bf16[5,64,512]{2,0,1:T(8,128)(2,1)}), bf16[5,64,512]{2,0,1:T(8,128)(2,1)S(1)}, u32[]{:S(2)}, u32[]{:S(2)}) async-start(bf16[5,64,512]{2,0,1:T(8,128)(2,1)} %copy.157), calls=%async_computation.2 | async-start | bytes 1048576 | tf_op jit(solution)/shard_map/all_to_all | solution.py:203
  495.4 25.7 %collective-permute-start.30 = (f32[512,8]{0,1:T(8,128)S(1)}, f32[512,8]{0,1:T(8,128)S(1)}, u32[]{:S(2)}, u32[]{:S(2)}) collective-permute-start(f32[512,8]{0,1:T(8,128)S(1)} %get-tuple-element.50), channel_id=1, source_target_pairs={{0,108},{4,112},{8,116},{12,120},{16,124},{20,128},{24,132},{28,13... | collective-permute-start | bytes 49160
  496.7 25.7 %collective-permute-start.29 = (f32[512,8]{0,1:T(8,128)S(1)}, f32[512,8]{0,1:T(8,128)S(1)}, u32[]{:S(2)}, u32[]{:S(2)}) collective-permute-start(f32[512,8]{0,1:T(8,128)S(1)} %get-tuple-element.50), channel_id=1, source_target_pairs={{0,104},{4,108},{8,112},{12,116},{16,120},{20,124},{24,128},{28,13... | collective-permute-start | bytes 49160
  498.0 25.7 %collective-permute-start.28 = (f32[512,8]{0,1:T(8,128)S(1)}, f32[512,8]{0,1:T(8,128)S(1)}, u32[]{:S(2)}, u32[]{:S(2)}) collective-permute-start(f32[512,8]{0,1:T(8,128)S(1)} %get-tuple-element.50), channel_id=1, source_target_pairs={{0,100},{4,104},{8,108},{12,112},{16,116},{20,120},{24,124},{28,12... | collective-permute-start | bytes 49160
  499.4 25.7 %collective-permute-start.27 = (f32[512,8]{0,1:T(8,128)S(1)}, f32[512,8]{0,1:T(8,128)S(1)}, u32[]{:S(2)}, u32[]{:S(2)}) collective-permute-start(f32[512,8]{0,1:T(8,128)S(1)} %get-tuple-element.50), channel_id=1, source_target_pairs={{0,96},{4,100},{8,104},{12,108},{16,112},{20,116},{24,120},{28,124... | collective-permute-start | bytes 49160
  500.7 25.7 %collective-permute-start.26 = (f32[512,8]{0,1:T(8,128)S(1)}, f32[512,8]{0,1:T(8,128)S(1)}, u32[]{:S(2)}, u32[]{:S(2)}) collective-permute-start(f32[512,8]{0,1:T(8,128)S(1)} %get-tuple-element.50), channel_id=1, source_target_pairs={{0,92},{4,96},{8,100},{12,104},{16,108},{20,112},{24,116},{28,120}... | collective-permute-start | bytes 49160
  547.0 20.1 %collective-permute-start.14 = (f32[512,8]{0,1:T(8,128)S(1)}, f32[512,8]{0,1:T(8,128)S(1)}, u32[]{:S(2)}, u32[]{:S(2)}) collective-permute-start(f32[512,8]{0,1:T(8,128)S(1)} %get-tuple-element.50), channel_id=1, source_target_pairs={{0,44},{4,48},{8,52},{12,56},{16,60},{20,64},{24,68},{28,72},{32,7... | collective-permute-start | bytes 49160
  550.1 18.9 %collective-permute-start.13 = (f32[512,8]{0,1:T(8,128)S(1)}, f32[512,8]{0,1:T(8,128)S(1)}, u32[]{:S(2)}, u32[]{:S(2)}) collective-permute-start(f32[512,8]{0,1:T(8,128)S(1)} %get-tuple-element.50), channel_id=1, source_target_pairs={{0,40},{4,44},{8,48},{12,52},{16,56},{20,60},{24,64},{28,68},{32,7... | collective-permute-start | bytes 49160
  552.7 19.7 %collective-permute-start.12 = (f32[512,8]{0,1:T(8,128)S(1)}, f32[512,8]{0,1:T(8,128)S(1)}, u32[]{:S(2)}, u32[]{:S(2)}) collective-permute-start(f32[512,8]{0,1:T(8,128)S(1)} %get-tuple-element.50), channel_id=1, source_target_pairs={{0,36},{4,40},{8,44},{12,48},{16,52},{20,56},{24,60},{28,64},{32,6... | collective-permute-start | bytes 49160
  557.9 34.6 %collective-permute-start.11 = (f32[512,8]{0,1:T(8,128)S(1)}, f32[512,8]{0,1:T(8,128)S(1)}, u32[]{:S(2)}, u32[]{:S(2)}) collective-permute-start(f32[512,8]{0,1:T(8,128)S(1)} %get-tuple-element.50), channel_id=1, source_target_pairs={{0,32},{4,36},{8,40},{12,44},{16,48},{20,52},{24,56},{28,60},{32,6... | collective-permute-start | bytes 49160
  562.3 34.5 %collective-permute-start.10 = (f32[512,8]{0,1:T(8,128)S(1)}, f32[512,8]{0,1:T(8,128)S(1)}, u32[]{:S(2)}, u32[]{:S(2)}) collective-permute-start(f32[512,8]{0,1:T(8,128)S(1)} %get-tuple-element.50), channel_id=1, source_target_pairs={{0,28},{4,32},{8,36},{12,40},{16,44},{20,48},{24,52},{28,56},{32,6... | collective-permute-start | bytes 49160
  567.1 32.3 %collective-permute-start.9 = (f32[512,8]{0,1:T(8,128)S(1)}, f32[512,8]{0,1:T(8,128)S(1)}, u32[]{:S(2)}, u32[]{:S(2)}) collective-permute-start(f32[512,8]{0,1:T(8,128)S(1)} %get-tuple-element.50), channel_id=1, source_target_pairs={{0,24},{4,28},{8,32},{12,36},{16,40},{20,44},{24,48},{28,52},{32,5... | collective-permute-start | bytes 49160
  569.0 32.3 %collective-permute-start.8 = (f32[512,8]{0,1:T(8,128)S(1)}, f32[512,8]{0,1:T(8,128)S(1)}, u32[]{:S(2)}, u32[]{:S(2)}) collective-permute-start(f32[512,8]{0,1:T(8,128)S(1)} %get-tuple-element.50), channel_id=1, source_target_pairs={{0,20},{4,24},{8,28},{12,32},{16,36},{20,40},{24,44},{28,48},{32,5... | collective-permute-start | bytes 49160
  572.4 30.3 %collective-permute-start.7 = (f32[512,8]{0,1:T(8,128)S(1)}, f32[512,8]{0,1:T(8,128)S(1)}, u32[]{:S(2)}, u32[]{:S(2)}) collective-permute-start(f32[512,8]{0,1:T(8,128)S(1)} %get-tuple-element.50), channel_id=1, source_target_pairs={{0,16},{4,20},{8,24},{12,28},{16,32},{20,36},{24,40},{28,44},{32,4... | collective-permute-start | bytes 49160
  592.5 22.3 %collective-permute-start.6 = (f32[512,8]{0,1:T(8,128)S(1)}, f32[512,8]{0,1:T(8,128)S(1)}, u32[]{:S(2)}, u32[]{:S(2)}) collective-permute-start(f32[512,8]{0,1:T(8,128)S(1)} %get-tuple-element.50), channel_id=1, source_target_pairs={{0,12},{4,16},{8,20},{12,24},{16,28},{20,32},{24,36},{28,40},{32,4... | collective-permute-start | bytes 49160
  596.8 19.3 %collective-permute-start.5 = (f32[512,8]{0,1:T(8,128)S(1)}, f32[512,8]{0,1:T(8,128)}, u32[]{:S(2)}, u32[]{:S(2)}) collective-permute-start(f32[512,8]{0,1:T(8,128)S(1)} %get-tuple-element.50), channel_id=1, source_target_pairs={{0,8},{4,12},{8,16},{12,20},{16,24},{20,28},{24,32},{28,36},{32,40... | collective-permute-start | bytes 49160
  610.1 32.1 %all-to-all-start.4 = ((bf16[20,16,512]{2,1,0:T(8,128)(2,1)}), bf16[20,16,512]{2,1,0:T(8,128)(2,1)}, u32[]{:S(2)}, u32[]{:S(2)}) async-start(bf16[20,16,512]{2,1,0:T(8,128)(2,1)} %convert_element_type.102), calls=%async_computation.4 | async-start | bytes 655360 | tf_op jit(solution)/shard_map/all_to_all | solution.py:208
  627.3 21.6 %collective-permute-start.59 = (f32[512,8]{0,1:T(8,128)S(1)}, f32[512,8]{0,1:T(8,128)S(1)}, u32[]{:S(2)}, u32[]{:S(2)}) collective-permute-start(f32[512,8]{0,1:T(8,128)S(1)} %get-tuple-element.51), channel_id=1, source_target_pairs={{0,96},{4,100},{8,104},{12,108},{16,112},{20,116},{24,120},{28,124... | collective-permute-start | bytes 49160
  628.9 21.4 %collective-permute-start.58 = (f32[512,8]{0,1:T(8,128)S(1)}, f32[512,8]{0,1:T(8,128)}, u32[]{:S(2)}, u32[]{:S(2)}) collective-permute-start(f32[512,8]{0,1:T(8,128)S(1)} %get-tuple-element.51), channel_id=1, source_target_pairs={{0,92},{4,96},{8,100},{12,104},{16,108},{20,112},{24,116},{28,120}... | collective-permute-start | bytes 49160
  632.5 19.2 %collective-permute-start.57 = (f32[512,8]{0,1:T(8,128)S(1)}, f32[512,8]{0,1:T(8,128)}, u32[]{:S(2)}, u32[]{:S(2)}) collective-permute-start(f32[512,8]{0,1:T(8,128)S(1)} %get-tuple-element.51), channel_id=1, source_target_pairs={{0,88},{4,92},{8,96},{12,100},{16,104},{20,108},{24,112},{28,116},... | collective-permute-start | bytes 49160
  634.4 19.1 %collective-permute-start.56 = (f32[512,8]{0,1:T(8,128)S(1)}, f32[512,8]{0,1:T(8,128)}, u32[]{:S(2)}, u32[]{:S(2)}) collective-permute-start(f32[512,8]{0,1:T(8,128)S(1)} %get-tuple-element.51), channel_id=1, source_target_pairs={{0,84},{4,88},{8,92},{12,96},{16,100},{20,104},{24,108},{28,112},{... | collective-permute-start | bytes 49160
  637.2 18.2 %collective-permute-start.55 = (f32[512,8]{0,1:T(8,128)S(1)}, f32[512,8]{0,1:T(8,128)}, u32[]{:S(2)}, u32[]{:S(2)}) collective-permute-start(f32[512,8]{0,1:T(8,128)S(1)} %get-tuple-element.51), channel_id=1, source_target_pairs={{0,80},{4,84},{8,88},{12,92},{16,96},{20,100},{24,104},{28,108},{3... | collective-permute-start | bytes 49160
  642.2 49.4 %all-to-all-start.5 = ((bf16[20,16,512]{2,1,0:T(8,128)(2,1)}), bf16[20,16,512]{2,1,0:T(8,128)(2,1)S(1)}, u32[]{:S(2)}, u32[]{:S(2)}) async-start(bf16[20,16,512]{2,1,0:T(8,128)(2,1)} %convert_element_type.105), calls=%async_computation.5 | async-start | bytes 655360 | tf_op jit(solution)/shard_map/all_to_all | solution.py:209
  648.9 27.2 %collective-permute-start.54 = (f32[512,8]{0,1:T(8,128)S(1)}, f32[512,8]{0,1:T(8,128)S(1)}, u32[]{:S(2)}, u32[]{:S(2)}) collective-permute-start(f32[512,8]{0,1:T(8,128)S(1)} %get-tuple-element.51), channel_id=1, source_target_pairs={{0,76},{4,80},{8,84},{12,88},{16,92},{20,96},{24,100},{28,104},{32... | collective-permute-start | bytes 49160
  650.3 29.8 %collective-permute-start.53 = (f32[512,8]{0,1:T(8,128)S(1)}, f32[512,8]{0,1:T(8,128)S(1)}, u32[]{:S(2)}, u32[]{:S(2)}) collective-permute-start(f32[512,8]{0,1:T(8,128)S(1)} %get-tuple-element.51), channel_id=1, source_target_pairs={{0,72},{4,76},{8,80},{12,84},{16,88},{20,92},{24,96},{28,100},{32,... | collective-permute-start | bytes 49160
  651.6 30.1 %collective-permute-start.52 = (f32[512,8]{0,1:T(8,128)S(1)}, f32[512,8]{0,1:T(8,128)}, u32[]{:S(2)}, u32[]{:S(2)}) collective-permute-start(f32[512,8]{0,1:T(8,128)S(1)} %get-tuple-element.51), channel_id=1, source_target_pairs={{0,68},{4,72},{8,76},{12,80},{16,84},{20,88},{24,92},{28,96},{32,1... | collective-permute-start | bytes 49160
  653.5 29.5 %collective-permute-start.51 = (f32[512,8]{0,1:T(8,128)S(1)}, f32[512,8]{0,1:T(8,128)}, u32[]{:S(2)}, u32[]{:S(2)}) collective-permute-start(f32[512,8]{0,1:T(8,128)S(1)} %get-tuple-element.51), channel_id=1, source_target_pairs={{0,64},{4,68},{8,72},{12,76},{16,80},{20,84},{24,88},{28,92},{32,9... | collective-permute-start | bytes 49160
  655.4 30.4 %collective-permute-start.50 = (f32[512,8]{0,1:T(8,128)S(1)}, f32[512,8]{0,1:T(8,128)}, u32[]{:S(2)}, u32[]{:S(2)}) collective-permute-start(f32[512,8]{0,1:T(8,128)S(1)} %get-tuple-element.51), channel_id=1, source_target_pairs={{0,60},{4,64},{8,68},{12,72},{16,76},{20,80},{24,84},{28,88},{32,9... | collective-permute-start | bytes 49160
  676.1 22.6 %collective-permute-start.49 = (f32[512,8]{0,1:T(8,128)S(1)}, f32[512,8]{0,1:T(8,128)S(1)}, u32[]{:S(2)}, u32[]{:S(2)}) collective-permute-start(f32[512,8]{0,1:T(8,128)S(1)} %get-tuple-element.51), channel_id=1, source_target_pairs={{0,56},{4,60},{8,64},{12,68},{16,72},{20,76},{24,80},{28,84},{32,8... | collective-permute-start | bytes 49160
  680.2 22.3 %collective-permute-start.48 = (f32[512,8]{0,1:T(8,128)S(1)}, f32[512,8]{0,1:T(8,128)S(1)}, u32[]{:S(2)}, u32[]{:S(2)}) collective-permute-start(f32[512,8]{0,1:T(8,128)S(1)} %get-tuple-element.51), channel_id=1, source_target_pairs={{0,52},{4,56},{8,60},{12,64},{16,68},{20,72},{24,76},{28,80},{32,8... | collective-permute-start | bytes 49160
  681.7 23.3 %collective-permute-start.47 = (f32[512,8]{0,1:T(8,128)S(1)}, f32[512,8]{0,1:T(8,128)S(1)}, u32[]{:S(2)}, u32[]{:S(2)}) collective-permute-start(f32[512,8]{0,1:T(8,128)S(1)} %get-tuple-element.51), channel_id=1, source_target_pairs={{0,48},{4,52},{8,56},{12,60},{16,64},{20,68},{24,72},{28,76},{32,8... | collective-permute-start | bytes 49160
  683.1 26.8 %collective-permute-start.46 = (f32[512,8]{0,1:T(8,128)S(1)}, f32[512,8]{0,1:T(8,128)S(1)}, u32[]{:S(2)}, u32[]{:S(2)}) collective-permute-start(f32[512,8]{0,1:T(8,128)S(1)} %get-tuple-element.51), channel_id=1, source_target_pairs={{0,44},{4,48},{8,52},{12,56},{16,60},{20,64},{24,68},{28,72},{32,7... | collective-permute-start | bytes 49160
  685.8 26.4 %collective-permute-start.45 = (f32[512,8]{0,1:T(8,128)S(1)}, f32[512,8]{0,1:T(8,128)S(1)}, u32[]{:S(2)}, u32[]{:S(2)}) collective-permute-start(f32[512,8]{0,1:T(8,128)S(1)} %get-tuple-element.51), channel_id=1, source_target_pairs={{0,40},{4,44},{8,48},{12,52},{16,56},{20,60},{24,64},{28,68},{32,7... | collective-permute-start | bytes 49160
  691.6 61.9 %all-to-all-start.6 = ((bf16[20,16,512]{2,1,0:T(8,128)(2,1)}), bf16[20,16,512]{2,1,0:T(8,128)(2,1)S(1)}, u32[]{:S(2)}, u32[]{:S(2)}) async-start(bf16[20,16,512]{2,1,0:T(8,128)(2,1)} %convert_element_type.109), calls=%async_computation.6 | async-start | bytes 655360 | tf_op jit(solution)/shard_map/all_to_all | solution.py:210
  698.7 63.4 %reduce-scatter.7.cloned.1.call-start = ((), (), s32[]{:S(2)}) async-start(), calls=%async_computation.10 | async-start | bytes 20480 | tf_op jit(solution)/shard_map/reduce_scatter | solution.py:236
  698.7 26.5 %collective-permute-start.44 = (f32[512,8]{0,1:T(8,128)S(1)}, f32[512,8]{0,1:T(8,128)S(1)}, u32[]{:S(2)}, u32[]{:S(2)}) collective-permute-start(f32[512,8]{0,1:T(8,128)S(1)} %get-tuple-element.51), channel_id=1, source_target_pairs={{0,36},{4,40},{8,44},{12,48},{16,52},{20,56},{24,60},{28,64},{32,6... | collective-permute-start | bytes 49160
  702.6 25.1 %collective-permute-start.43 = (f32[512,8]{0,1:T(8,128)S(1)}, f32[512,8]{0,1:T(8,128)S(1)}, u32[]{:S(2)}, u32[]{:S(2)}) collective-permute-start(f32[512,8]{0,1:T(8,128)S(1)} %get-tuple-element.51), channel_id=1, source_target_pairs={{0,32},{4,36},{8,40},{12,44},{16,48},{20,52},{24,56},{28,60},{32,6... | collective-permute-start | bytes 49160
  705.1 24.1 %collective-permute-start.42 = (f32[512,8]{0,1:T(8,128)S(1)}, f32[512,8]{0,1:T(8,128)S(1)}, u32[]{:S(2)}, u32[]{:S(2)}) collective-permute-start(f32[512,8]{0,1:T(8,128)S(1)} %get-tuple-element.51), channel_id=1, source_target_pairs={{0,28},{4,32},{8,36},{12,40},{16,44},{20,48},{24,52},{28,56},{32,6... | collective-permute-start | bytes 49160
  709.9 24.9 %collective-permute-start.41 = (f32[512,8]{0,1:T(8,128)S(1)}, f32[512,8]{0,1:T(8,128)}, u32[]{:S(2)}, u32[]{:S(2)}) collective-permute-start(f32[512,8]{0,1:T(8,128)S(1)} %get-tuple-element.51), channel_id=1, source_target_pairs={{0,24},{4,28},{8,32},{12,36},{16,40},{20,44},{24,48},{28,52},{32,5... | collective-permute-start | bytes 49160
  712.3 23.8 %collective-permute-start.40 = (f32[512,8]{0,1:T(8,128)S(1)}, f32[512,8]{0,1:T(8,128)}, u32[]{:S(2)}, u32[]{:S(2)}) collective-permute-start(f32[512,8]{0,1:T(8,128)S(1)} %get-tuple-element.51), channel_id=1, source_target_pairs={{0,20},{4,24},{8,28},{12,32},{16,36},{20,40},{24,44},{28,48},{32,5... | collective-permute-start | bytes 49160
  725.3 25.0 %collective-permute-start.3 = (f32[5,15,512]{2,1,0:T(8,128)S(1)}, f32[5,15,512]{2,1,0:T(8,128)S(1)}, u32[]{:S(2)}, u32[]{:S(2)}) collective-permute-start(f32[5,15,512]{2,1,0:T(8,128)S(1)} %copy-done.31), channel_id=1, source_target_pairs={{4,0},{8,4},{12,8},{16,12},{20,16},{24,20},{28,24},{32,28},{36,32}... | collective-permute-start | bytes 460808 | tf_op jit(solution)/shard_map/ppermute | solution.py:16
  739.8 51.9 %reduce-scatter.9.cloned.1.call-start = ((), (), s32[]{:S(2)}) async-start(), calls=%async_computation.11 | async-start | bytes 20480 | tf_op jit(solution)/shard_map/reduce_scatter | solution.py:237
  (134 other events, 2658.0 us)
Sparse Core Ops, SparseCore 0:
  739.9 22.0 reduce-scatter.6
  765.7 25.9 reduce-scatter.8
where the time goes:
time: 810 us; the launch traced here: 799 us
  blocking collectives  355 us (44%)
  starting transfers between devices  256 us (32%)
  local copies, waits for them, and re-layouts  64.9 us (8%)
  waiting for transfers between devices  41 us (5%)
  matrix products  37.2 us (5%)
  other arithmetic  27.2 us (3%)
  between operations  17.4 us (2%)
    unnamed x1, blocking collectives  311 us
    unnamed x64, starting transfers between devices  173 us
    unnamed x223, local copies, waits for them, and re-layouts  35.6 us
    ppermute x4, starting transfers between devices, passed_along(): lax.ppermute(value, axis, [(source, source + steps) for source in range(l...  32.1 us
    reduce_scatter x1, waiting for transfers between devices, per_device(): lax.psum_scatter(partial_sums[1], 'series', scatter_dimension=0, tiled=True)  29.6 us
    all_gather x1, blocking collectives, per_device(): lax.all_gather(out_time, 'series', axis=0, tiled=True)  26.7 us
    all_gather x1, blocking collectives, per_device(): lax.all_gather(out_group, 'series', axis=0, tiled=True)  17.9 us
  transfers between devices with their start and end apart: 78, of which 5 were waited for; matrix products, arithmetic and copies ran while one was open for 55% of the time, Pallas kernels for 0%

commit v1 on v0

v1 whole, which is shorter than its diff:
```python
import functools

import jax
import jax.numpy as jnp
import numpy as np
from jax import lax
from jax.experimental import pallas as pl
from jax.experimental.pallas import tpu as pltpu
from jax.sharding import PartitionSpec as P

HEAD_DIM = 64
BAND = 16
QUAD = 4
MASKED = -1e30
F32 = jnp.float32
BF16 = jnp.bfloat16
NT = (((1,), (1,)), ((), ()))
NN = (((1,), (0,)), ((), ()))
TN = (((0,), (0,)), ((), ()))


def dot(left, right, dims):
    return lax.dot_general(left, right, dims, preferred_element_type=F32)


def call(body, out_shape, operands, flops, size, smem=(), aliases=None, scratch=()):
    space = [
        pl.BlockSpec(memory_space=pltpu.SMEM if index in smem else pltpu.VMEM)
        for index in range(len(operands))
    ]
    single = isinstance(out_shape, jax.ShapeDtypeStruct)
    out_specs = (
        pl.BlockSpec(memory_space=pltpu.VMEM)
        if single
        else [pl.BlockSpec(memory_space=pltpu.VMEM)] * len(out_shape)
    )
    return pl.pallas_call(
        body,
        out_shape=out_shape,
        in_specs=space,
        out_specs=out_specs,
        scratch_shapes=list(scratch),
        input_output_aliases=aliases or {},
        compiler_params=pltpu.CompilerParams(vmem_limit_bytes=48 * 1024 * 1024),
        cost_estimate=pl.CostEstimate(flops=flops, bytes_accessed=size, transcendentals=0),
    )(*operands)


def shape(dims, dtype):
    return jax.ShapeDtypeStruct(dims, dtype)


def stacked(rows):
    lane = lax.broadcasted_iota(jnp.int32, rows.shape, 1) // HEAD_DIM
    zero = jnp.zeros_like(rows)
    return jnp.concatenate([jnp.where(lane == h, rows, zero) for h in range(QUAD)], axis=0)


def unstacked(rows):
    count = rows.shape[0] // QUAD
    low = lax.broadcasted_iota(jnp.int32, (count, 2 * HEAD_DIM), 1) < HEAD_DIM
    parts = []
    for pair in range(QUAD // 2):
        lanes = slice(2 * HEAD_DIM * pair, 2 * HEAD_DIM * (pair + 1))
        first = rows[2 * pair * count : (2 * pair + 1) * count, lanes]
        second = rows[(2 * pair + 1) * count : (2 * pair + 2) * count, lanes]
        parts.append(jnp.where(low, first, second))
    return jnp.concatenate(parts, axis=1)


def column_softmax(scores, keep):
    scores = jnp.where(keep, scores * HEAD_DIM ** (-0.5), MASKED)
    weights = jnp.exp(scores - jnp.max(scores, axis=0, keepdims=True))
    return weights * (1.0 / jnp.sum(weights, axis=0, keepdims=True))


def backward(prob, query_stack, key, value, grad_stack):
    grad_prob = dot(value, grad_stack, NT).astype(BF16).astype(F32)
    centred = grad_prob - jnp.sum(grad_prob * prob, axis=0, keepdims=True)
    grad_score = prob * centred * HEAD_DIM ** (-0.5)
    high = grad_score.astype(BF16)
    low = (grad_score - high.astype(F32)).astype(BF16)
    grad_query = dot(high, key, TN) + dot(low, key, TN)
    grad_key = dot(high, query_stack, NN) + dot(low, query_stack, NN)
    grad_value = dot(prob.astype(BF16), grad_stack, NN)
    return grad_query, grad_key, grad_value


def term_of(spread_ref, cot, mixed, scale, out_ref):
    rows = dot(spread_ref[...], cot, NT).astype(BF16)
    term = dot(rows, mixed, NN) * scale
    for part in range(out_ref.shape[0]):
        out_ref[part] = term[:, 128 * part : 128 * (part + 1)].astype(BF16)


def pack_body(q_ref, k_ref, v_ref, c_ref, out_ref):
    ser = q_ref.shape[0]
    start = 0
    for ref in (q_ref, k_ref, v_ref, c_ref):
        width = ref.shape[2]
        for s in range(ser):
            for j in range(out_ref.shape[0]):
                out_ref[j, 16 * s : 16 * (s + 1), start : start + width] = ref[
                    s, 16 * j : 16 * (j + 1), :
                ]
        start += width


def unpack_body(in_ref, q_ref, k_ref, v_ref):
    ser = q_ref.shape[0]
    for index, ref in enumerate((q_ref, k_ref, v_ref)):
        width = ref.shape[2]
        for s in range(ser):
            for j in range(in_ref.shape[0]):
                ref[s, 16 * j : 16 * (j + 1), :] = in_ref[
                    j, 16 * s : 16 * (s + 1), width * index : width * (index + 1)
                ]


def time_forward_body(
    scale, q_ref, k_ref, v_ref, rim_ref, c_ref, spread_ref, band_ref, first_ref, prob_ref, term_ref, mixed
):
    ser, rows, width = q_ref.shape
    keys = rows + BAND
    lanes = QUAD * HEAD_DIM
    key_pos = lax.broadcasted_iota(jnp.int32, (keys, QUAD * rows), 0)
    column = lax.broadcasted_iota(jnp.int32, (keys, QUAD * rows), 1)
    offset = lax.rem(column, rows) + BAND - key_pos
    head = column // rows
    inside = key_pos >= jnp.where(first_ref[0] == 0, BAND, 0)
    for quad in range(width // lanes):
        band = jnp.where(
            head < 2,
            jnp.where(head == 0, band_ref[QUAD * quad], band_ref[QUAD * quad + 1]),
            jnp.where(head == 2, band_ref[QUAD * quad + 2], band_ref[QUAD * quad + 3]),
        )
        keep = (offset >= 0) & (offset < band) & inside
        cut = slice(lanes * quad, lanes * (quad + 1))
        for s in range(ser):
            key = jnp.concatenate([rim_ref[0, s, :, cut], k_ref[s, :, cut]], axis=0)
            value = jnp.concatenate([rim_ref[1, s, :, cut], v_ref[s, :, cut]], axis=0)
            prob = column_softmax(dot(key, stacked(q_ref[s, :, cut]), NT), keep)
            prob_ref[s, quad] = prob
            out = unstacked(dot(prob.astype(BF16), value, TN))
            mixed[rows * s : rows * (s + 1), cut] = out.astype(BF16)
    cot = c_ref[...].reshape(ser * rows, c_ref.shape[2])
    term_of(spread_ref, cot, mixed[...], scale, term_ref)


def time_backward_body(
    prob_ref, q_ref, k_ref, v_ref, rim_ref, c_ref, w_ref, gq_ref, gk_ref, gv_ref, tail_ref, rimg_ref, grad
):
    ser, rows, width = q_ref.shape
    lanes = QUAD * HEAD_DIM
    cot = c_ref[...].reshape(ser * rows, c_ref.shape[2])
    for j in range(w_ref.shape[0]):
        grad[:, 128 * j : 128 * (j + 1)] = dot(cot, w_ref[j, :128, :], NT).astype(BF16)
    for quad in range(width // lanes):
        cut = slice(lanes * quad, lanes * (quad + 1))
        for s in range(ser):
            key = jnp.concatenate([rim_ref[0, s, :, cut], k_ref[s, :, cut]], axis=0)
            value = jnp.concatenate([rim_ref[1, s, :, cut], v_ref[s, :, cut]], axis=0)
            gq, gk, gv = backward(
                prob_ref[s, quad],
                stacked(q_ref[s, :, cut]),
                key,
                value,
                stacked(grad[rows * s : rows * (s + 1), cut]),
            )
            gq_ref[s, :, cut] = unstacked(gq).astype(BF16)
            for index, (result, ref) in enumerate(((gk, gk_ref), (gv, gv_ref))):
                rimg_ref[index, s, :, cut] = result[:BAND]
                ref[s, :, cut] = result[BAND:].astype(BF16)
                tail_ref[index, s, :, cut] = result[rows:]


def time_join_body(gk_in, gv_in, tail_ref, got_ref, gk_ref, gv_ref):
    rows = gk_in.shape[1]
    for index, (source, ref) in enumerate(((gk_in, gk_ref), (gv_in, gv_ref))):
        ref[:, : rows - BAND, :] = source[:, : rows - BAND, :]
        ref[:, rows - BAND :, :] = (tail_ref[index] + got_ref[index]).astype(BF16)


def group_body(scale, x_ref, w_ref, spread_ref, idk_ref, idq_ref, out_ref, term_ref, grad, mixed, res):
    total = x_ref.shape[0]
    patches = 16
    series = total // patches
    width = w_ref.shape[0] * 128
    lanes = QUAD * HEAD_DIM
    half = patches // 2
    cot = x_ref[:, 3 * width :]
    for j in range(w_ref.shape[0]):
        grad[:, 128 * j : 128 * (j + 1)] = dot(cot, w_ref[j, 128:, :], NT).astype(BF16)
    keep = idk_ref[...] == idq_ref[...]

    def rows_of(whole, part):
        cube = whole.astype(F32).reshape(series, patches, whole.shape[1])
        return cube[:, half * part : half * (part + 1)].reshape(-1, whole.shape[1]).astype(BF16)

    for quad in range(width // lanes):
        cut = [slice(width * n + lanes * quad, width * n + lanes * (quad + 1)) for n in range(3)]
        for part in range(2):
            query = stacked(rows_of(x_ref[:, cut[0]], part))
            key = rows_of(x_ref[:, cut[1]], part)
            value = rows_of(x_ref[:, cut[2]], part)
            prob = column_softmax(dot(key, query, NT), keep)
            out = unstacked(dot(prob.astype(BF16), value, TN))
            grad_stack = stacked(rows_of(grad[:, cut[0]], part))
            gq, gk, gv = backward(prob, query, key, value, grad_stack)
            place = slice(half * part, half * (part + 1))
            for index, result in enumerate((unstacked(gq), gk, gv, out)):
                spot = slice(width * index + lanes * quad, width * index + lanes * (quad + 1))
                res[:, place, spot] = result.reshape(series, half, lanes)
    out_ref[...] = res[:, :, : 3 * width].reshape(total, 3 * width).astype(BF16)
    mixed[...] = res[:, :, 3 * width :].reshape(total, width).astype(BF16)
    term_of(spread_ref, cot, mixed[...], scale, term_ref)


def sum_body(in_ref, out_ref):
    chunks = in_ref.shape[0] // 8
    total = jnp.sum(in_ref[...].astype(F32).reshape(chunks, 8, 128), axis=0)
    out_ref[...] = jnp.transpose(total)[:, : out_ref.shape[1]]


def per_device(
    time_query,
    time_key,
    time_value,
    group_query,
    group_key,
    group_value,
    out_time,
    out_group,
    series_group,
    band_width,
    cotangent,
):
    ser, rows, width = time_query.shape
    model = cotangent.shape[2]
    parts = lax.axis_size("series")
    count = lax.axis_size("tm")
    columns = model // count
    scale = float(ser * parts * rows * count) ** (-0.5)
    place = lax.axis_index("tm")
    patches = rows // parts

    rim = jnp.stack([time_key[:, rows - BAND :], time_value[:, rows - BAND :]])
    rim = lax.ppermute(rim, "tm", [(i, i + 1) for i in range(count - 1)])

    packed = call(
        pack_body,
        shape((parts, ser * patches, 3 * width + model), BF16),
        (group_query, group_key, group_value, cotangent),
        0,
        3_000_000,
    )
    moved = lax.all_to_all(packed, "series", 0, 0, tiled=True)
    weights = lax.all_gather(jnp.concatenate([out_time, out_group], axis=0), "series", axis=0)

    spread = np.zeros((8 * count, model), np.float32)
    for i in range(count):
        for e in range(columns):
            spread[8 * i + e, columns * i + e] = 1
    spread = jnp.asarray(spread, BF16)

    ident = series_group[:, None] * (patches // 2) + jnp.arange(patches // 2, dtype=jnp.int32)[None]
    ident = ident.reshape(-1)
    id_key = ident[:, None]
    id_query = jnp.tile(ident, QUAD)[None]

    quads = width // (QUAD * HEAD_DIM)
    prob, term_time = call(
        functools.partial(time_forward_body, scale),
        (
            shape((ser, quads, rows + BAND, QUAD * rows), F32),
            shape((parts, 8 * count, 128), BF16),
        ),
        (time_query, time_key, time_value, rim, cotangent, spread, band_width, place.reshape(1)),
        2_000_000_000,
        6_000_000,
        smem=(6, 7),
        scratch=[pltpu.VMEM((ser * rows, width), BF16)],
    )
    got_time = lax.all_to_all(
        term_time.reshape(parts * count, 8, 128), ("series", "tm"), 0, 0, tiled=True
    )
    grad_wt = call(
        sum_body, shape((128, columns), F32), (got_time.reshape(-1, 128),), 0, 1_000_000
    )

    back, term_group = call(
        functools.partial(group_body, scale),
        (
            shape((parts * ser * patches, 3 * width), BF16),
            shape((parts, 8 * count, 128), BF16),
        ),
        (
            moved.reshape(parts * ser * patches, 3 * width + model),
            weights,
            spread,
            id_key,
            id_query,
        ),
        4_000_000_000,
        6_000_000,
        scratch=[
            pltpu.VMEM((parts * ser * patches, width), BF16),
            pltpu.VMEM((parts * ser * patches, width), BF16),
            pltpu.VMEM((parts * ser, patches, 4 * width), F32),
        ],
    )
    returned = lax.all_to_all(
        back.reshape(parts, ser * patches, 3 * width), "series", 0, 0, tiled=True
    )
    got_group = lax.all_to_all(
        term_group.reshape(parts * count, 8, 128), ("series", "tm"), 0, 0, tiled=True
    )

    grad_tq, grad_tk, grad_tv, tail, rim_grad = call(
        time_backward_body,
        (
            shape((ser, rows, width), BF16),
            shape((ser, rows, width), BF16),
            shape((ser, rows, width), BF16),
            shape((2, ser, BAND, width), F32),
            shape((2, ser, BAND, width), F32),
        ),
        (prob, time_query, time_key, time_value, rim, cotangent, weights),
        2_000_000_000,
        6_000_000,
        scratch=[pltpu.VMEM((ser * rows, width), BF16)],
    )
    rim_back = lax.ppermute(rim_grad, "tm", [(i + 1, i) for i in range(count - 1)])
    grad_tk, grad_tv = call(
        time_join_body,
        (shape((ser, rows, width), BF16), shape((ser, rows, width), BF16)),
        (grad_tk, grad_tv, tail, rim_back),
        0,
        2_000_000,
    )
    grad_wg = call(
        sum_body, shape((128, columns), F32), (got_group.reshape(-1, 128),), 0, 1_000_000
    )
    grad_gq, grad_gk, grad_gv = call(
        unpack_body,
        (shape((ser, rows, width), BF16),) * 3,
        (returned,),
        0,
        2_000_000,
    )
    return (grad_tq, grad_tk, grad_tv, grad_gq, grad_gk, grad_gv, grad_wt, grad_wg)


def solution(mesh):
    rows = P("series", "tm", None)
    return jax.shard_map(
        per_device,
        mesh=mesh,
        in_specs=(rows,) * 6 + (P("series", None),) * 2 + (P(), P(), rows),
        out_specs=(rows,) * 6 + (P("series", "tm"),) * 2,
        check_vma=False,
    )
```

time: 810 us -> 205 us (0.25); the launches traced: 799 us -> 204 us
  blocking collectives: 355 us -> 28.3 us
  starting transfers between devices: 256 us -> 73.6 us
  local copies, waits for them, and re-layouts: 64.9 us -> 23.1 us
  matrix products: 37.2 us -> 0 us
  other arithmetic: 27.2 us -> 1.89 us
  Pallas kernels: 0 us -> 20.5 us
    unnamed x1 -> x0, blocking collectives: 311 us -> none
    unnamed x64 -> x0, starting transfers between devices: 173 us -> none
    all_gather x2 -> x0, blocking collectives: 44.6 us -> none  [the longest x1 26.7 us: per_device(): lax.all_gather(out_time, 'series', axis=0, tiled=True)]
    reduce_scatter x2 -> x0, waiting for transfers between devices: 37.4 us -> none  [the longest x1 29.6 us: per_device(): lax.psum_scatter(partial_sums[1], 'series', scatter_dimension=0, tiled=True)]
    dot_general x16 -> x0, matrix products: 37.2 us -> none  [the longest x1 7.29 us: temporal_attend(): jnp.einsum('shti,sthd->sihd', rounded, grad_heads, preferred_element_type...]
    all_to_all x8 -> x3, waiting for transfers between devices: 3.31 us -> 36.3 us  [the longest x1 22.9 us: per_device(): lax.all_to_all(term_time.reshape(parts * count, 8, 128), ('series', 'tm')...]
    all_to_all x0 -> x1, blocking collectives: none -> 28.3 us  [per_device(): lax.all_to_all(back.reshape(parts, ser * patches, 3 * width), 'series', 0...]
    sub x4 -> x0, other arithmetic: 24 us -> none  [the longest x1 14.8 us: score_grad(): grad_inner - jnp.sum(grad_inner * probabilities, axis=-1, keepdims=True)]
  transfers between devices with their start and end apart: 78 -> 6, of which waited for: 5 -> 5; matrix products, arithmetic and copies ran while one was open for 55% -> 1% of each run, Pallas kernels for 0% -> 9%
where the time goes in v1:
time: 205 us; the launch traced here: 204 us
  starting transfers between devices  73.6 us (36%)
  waiting for transfers between devices  42 us (20%)
  blocking collectives  28.3 us (14%)
  local copies, waits for them, and re-layouts  23.1 us (11%)
  Pallas kernels  20.5 us (10%)
  between operations  14.3 us (7%)
    all_to_all x1, starting transfers between devices, per_device(): lax.all_to_all(term_time.reshape(parts * count, 8, 128), ('series', 'tm')...  40.9 us
    all_to_all x1, blocking collectives, per_device(): lax.all_to_all(back.reshape(parts, ser * patches, 3 * width), 'series', 0...  28.3 us
    all_to_all x1, waiting for transfers between devices, per_device(): lax.all_to_all(term_time.reshape(parts * count, 8, 128), ('series', 'tm')...  22.9 us
    unnamed x60, local copies, waits for them, and re-layouts  22.8 us
    pallas_call x8, Pallas kernels, call(): pl.pallas_call(body, out_shape=out_shape, in_specs=space, out_specs=out_s...  20.5 us
    all_to_all x1, starting transfers between devices, per_device(): lax.all_to_all(term_group.reshape(parts * count, 8, 128), ('series', 'tm'...  11.4 us
    all_to_all x1, starting transfers between devices, per_device(): moved = lax.all_to_all(packed, 'series', 0, 0, tiled=True)  11 us
    all_to_all x1, waiting for transfers between devices, per_device(): moved = lax.all_to_all(packed, 'series', 0, 0, tiled=True)  9.33 us
  transfers between devices with their start and end apart: 6, of which 5 were waited for; matrix products, arithmetic and copies ran while one was open for 1% of the time, Pallas kernels for 9%

profile of v1, /device:TPU:1, one launch (start us, length us, event | category | flops | bytes accessed | tf_op | source)
XLA Modules:
  0.0 203.6 jit_solution(9368207551451529358)
XLA Ops:
  7.2 1.0 copy-done.3
  8.2 1.0 copy-done.10
  9.2 1.0 copy-done.11
  10.1 1.0 copy-done.12
  11.1 1.2 shard_map.182
  12.3 11.0 %all-to-all-start = ((bf16[4,80,2304]{2,1,0:T(8,128)(2,1)}), bf16[4,80,2304]{2,1,0:T(8,128)(2,1)S(1)}, u32[]{:S(2)}, u32[]{:S(2)}) async-start(bf16[4,80,2304]{2,1,0:T(8,128)(2,1)} %shard_map.182), calls=%async_computation | async-start | bytes 2949120 | tf_op jit(solution)/shard_map/all_to_all | solution.py:257
  23.3 0.0 all-gather.3.cloned.1.call-start
  23.4 1.8 pad_maximum_fusion
  25.3 4.0 %collective-permute-start = (bf16[2,5,16,512]{3,2,1,0:T(8,128)(2,1)S(1)}, bf16[2,5,16,512]{3,2,1,0:T(8,128)(2,1)S(1)}, u32[]{:S(2)}, u32[]{:S(2)}) collective-permute-start(bf16[2,5,16,512]{3,2,1,0:T(8,128)(2,1)S(1)} %pad_maximum_fusion.1), channel_id=1, source_target_pairs={{0,4},{4,8},{8,12},{12,16},{16,20},{20,24},{24,28},{28,32},{32,36}... | collective-permute-start | bytes 491528 | tf_op jit(solution)/shard_map/ppermute | solution.py:248
  29.3 2.2 %collective-permute-done.rim_ref = bf16[2,5,16,512]{3,2,1,0:T(8,128)(2,1)S(1)} collective-permute-done((bf16[2,5,16,512]{3,2,1,0:T(8,128)(2,1)S(1)}, bf16[2,5,16,512]{3,2,1,0:T(8,128)(2,1)S(1)}, u32[]{:S(2)}, u32[]{:S(2)}) %collective-permute-start) | collective-permute-done | bytes 163872 | tf_op jit(solution)/shard_map/ppermute | solution.py:248
  31.6 1.5 copy-done.24
  33.1 3.3 %shard_map.179 = (f32[5,2,80,256]{3,2,1,0:T(8,128)S(1)}, bf16[4,1024,128]{2,1,0:T(8,128)(2,1)S(1)}) custom-call(bf16[5,64,512]{2,1,0:T(8,128)(2,1)S(1)} %copy-done.19, bf16[5,64,512]{2,1,0:T(8,128)(2,1)S(1)} %copy-done.13, bf16[5,64,512]{2,1,0:T(8,128)(2,1)S(1)} %copy-done.15, bf16[2,5,16,512]{3,2,1,0:T(8,128)(2,1)S(1)} %collective-permute-done.rim_ref, ...), custom_call_target="tpu_custom_call" | custom-call | flops 2000000000 | bytes 6000000 | tf_op jit(solution)/shard_map/pallas_call | solution.py:37
  36.3 1.0 copy-done.1
  37.3 0.9 copy-done.25
  38.2 9.3 %all-to-all-done = bf16[4,80,2304]{2,1,0:T(8,128)(2,1)S(1)} async-done(((bf16[4,80,2304]{2,1,0:T(8,128)(2,1)}), bf16[4,80,2304]{2,1,0:T(8,128)(2,1)S(1)}, u32[]{:S(2)}, u32[]{:S(2)}) %all-to-all-start) | async-done | bytes 1474592 | tf_op jit(solution)/shard_map/all_to_all | solution.py:257
  47.6 40.9 %all-to-all-start.2 = ((bf16[512,8,128]{2,1,0:T(8,128)(2,1)}), bf16[512,8,128]{2,1,0:T(8,128)(2,1)S(1)}, u32[]{:S(2)}, u32[]{:S(2)}) async-start(bf16[512,8,128]{2,1,0:T(8,128)(2,1)} %bitcast.16), calls=%async_computation.2 | async-start | bytes 2097152 | tf_op jit(solution)/shard_map/all_to_all | solution.py:284
  88.4 0.1 iota_add_fusion
  88.5 0.1 add.34
  88.6 0.1 add.35.idk_ref
  88.7 0.1 broadcast_in_dim_tile.3.idq_ref
  88.8 1.4 copy-done.17
  90.2 6.9 %shard_map.183 = (bf16[320,1536]{1,0:T(8,128)(2,1)S(1)}, bf16[4,1024,128]{2,1,0:T(8,128)(2,1)S(1)}) custom-call(bf16[320,2304]{1,0:T(8,128)(2,1)S(1)} %bitcast.14, bf16[4,256,768]{2,1,0:T(8,128)(2,1)S(1)} %bitcast.18, bf16[1024,768]{1,0:T(8,128)(2,1)} %constant.10.clone.spread_ref, s32[160,1]{1,0:T(8,128)S(1)} %add.35.idk_ref, ...), custom_call_target="tpu_custom_call" | custom-call | flops 4000000000 | bytes 6000000 | tf_op jit(solution)/shard_map/pallas_call | solution.py:37
  97.1 1.0 copy-done
  98.1 1.0 copy-done.2
  99.1 22.9 %all-to-all-done.2 = bf16[512,8,128]{2,1,0:T(8,128)(2,1)S(1)} async-done(((bf16[512,8,128]{2,1,0:T(8,128)(2,1)}), bf16[512,8,128]{2,1,0:T(8,128)(2,1)S(1)}, u32[]{:S(2)}, u32[]{:S(2)}) %all-to-all-start.2) | async-done | bytes 1048608 | tf_op jit(solution)/shard_map/all_to_all | solution.py:284
  122.1 28.3 %all_to_all.20.in_ref = bf16[4,80,1536]{2,1,0:T(8,128)(2,1)S(1)} all-to-all(bf16[4,80,1536]{2,1,0:T(8,128)(2,1)} %bitcast.17), channel_id=1, replica_groups=mesh['tm'=128,'series'=4] {'series'}, dimensions={0} | all-to-all | bytes 1966080 | tf_op jit(solution)/shard_map/all_to_all | solution.py:312
  150.3 11.4 %all-to-all-start.3 = ((bf16[512,8,128]{2,1,0:T(8,128)(2,1)}), bf16[512,8,128]{2,1,0:T(8,128)(2,1)S(1)}, u32[]{:S(2)}, u32[]{:S(2)}) async-start(bf16[512,8,128]{2,1,0:T(8,128)(2,1)} %bitcast.15), calls=%async_computation.3 | async-start | bytes 2097152 | tf_op jit(solution)/shard_map/all_to_all | solution.py:315
  161.7 1.0 copy-done.5
  162.7 1.0 copy-done.14
  163.7 1.0 copy-done.16
  164.7 1.4 copy-done.18
  166.1 1.0 copy-done.20
  167.1 0.9 copy-done.22
  168.0 1.1 copy-done.26
  169.1 5.0 %shard_map.180 = (bf16[5,64,512]{2,1,0:T(8,128)(2,1)}, bf16[5,64,512]{2,1,0:T(8,128)(2,1)S(1)}, bf16[5,64,512]{2,1,0:T(8,128)(2,1)S(1)}, f32[2,5,16,512]{3,2,1,0:T(8,128)S(1)}, f32[2,5,16,512]{3,2,1,0:T(8,128)}) custom-call(f32[5,2,80,256]{3,2,1,0:T(8,128)S(1)} %copy-done.26, bf16[5,64,512]{2,1,0:T(8,128)(2,1)S(1)} %copy-done.20, ...), custom_call_target="tpu_custom_call" | custom-call | flops 2000000000 | bytes 6000000 | tf_op jit(solution)/shard_map/pallas_call | solution.py:37
  174.1 0.7 copy-done.6
  174.9 0.7 copy-done.8
  175.6 6.3 %collective-permute-start.1 = (f32[2,5,16,512]{3,2,1,0:T(8,128)}, f32[2,5,16,512]{3,2,1,0:T(8,128)}, u32[]{:S(2)}, u32[]{:S(2)}) collective-permute-start(f32[2,5,16,512]{3,2,1,0:T(8,128)} %get-tuple-element.27), channel_id=1, source_target_pairs={{4,0},{8,4},{12,8},{16,12},{20,16},{24,20},{28,24},{32,28},{36,32}... | collective-permute-start | bytes 983048 | tf_op jit(solution)/shard_map/ppermute | solution.py:333
  181.9 0.6 shard_map.185
  182.6 0.7 copy.23
  183.2 3.4 %collective-permute-done.1.got_ref = f32[2,5,16,512]{3,2,1,0:T(8,128)} collective-permute-done((f32[2,5,16,512]{3,2,1,0:T(8,128)}, f32[2,5,16,512]{3,2,1,0:T(8,128)}, u32[]{:S(2)}, u32[]{:S(2)}) %collective-permute-start.1) | collective-permute-done | bytes 327712 | tf_op jit(solution)/shard_map/ppermute | solution.py:333
  186.7 1.0 copy-done.7
  187.7 1.0 copy-done.9
  188.6 1.9 shard_map.181
  190.5 1.0 shard_map.184
  191.5 4.0 %all-to-all-done.3 = bf16[512,8,128]{2,1,0:T(8,128)(2,1)S(1)} async-done(((bf16[512,8,128]{2,1,0:T(8,128)(2,1)}), bf16[512,8,128]{2,1,0:T(8,128)(2,1)S(1)}, u32[]{:S(2)}, u32[]{:S(2)}) %all-to-all-start.3) | async-done | bytes 1048608 | tf_op jit(solution)/shard_map/all_to_all | solution.py:315
  195.5 0.6 shard_map.186
  196.1 0.7 copy.24
  (43 shorter events, 0.1 us)
Async XLA Ops:
  7.2 1.0 copy-start.3
  8.2 1.0 copy-start.10
  9.2 1.0 copy-start.11
  10.1 1.0 copy-start.12
  12.3 11.0 %copy-start.27 = (bf16[128,768]{1,0:T(8,128)(2,1)S(1)}, bf16[128,768]{1,0:T(8,128)(2,1)}, u32[]{:S(2)}) copy-start(bf16[128,768]{1,0:T(8,128)(2,1)} %param.19) | copy-start | bytes 589828
  12.3 12.9 %copy-start.13 = (bf16[5,64,512]{2,1,0:T(8,128)(2,1)S(1)}, bf16[5,64,512]{2,1,0:T(8,128)(2,1)}, u32[]{:S(2)}) copy-start(bf16[5,64,512]{2,1,0:T(8,128)(2,1)} %k_ref.4) | copy-start | bytes 983044
  12.3 12.9 %copy-start.15 = (bf16[5,64,512]{2,1,0:T(8,128)(2,1)S(1)}, bf16[5,64,512]{2,1,0:T(8,128)(2,1)}, u32[]{:S(2)}) copy-start(bf16[5,64,512]{2,1,0:T(8,128)(2,1)} %v_ref.4) | copy-start | bytes 983044
  12.3 35.2 %all-to-all-start = ((bf16[4,80,2304]{2,1,0:T(8,128)(2,1)}), bf16[4,80,2304]{2,1,0:T(8,128)(2,1)S(1)}, u32[]{:S(2)}, u32[]{:S(2)}) async-start(bf16[4,80,2304]{2,1,0:T(8,128)(2,1)} %shard_map.182), calls=%async_computation | async-start | bytes 2949120 | tf_op jit(solution)/shard_map/all_to_all | solution.py:257
  23.3 8.3 %copy-start.4 = (bf16[5,64,768]{2,1,0:T(8,128)(2,1)S(1)}, bf16[5,64,768]{2,1,0:T(8,128)(2,1)}, u32[]{:S(2)}) copy-start(bf16[5,64,768]{2,1,0:T(8,128)(2,1)} %c_ref.5) | copy-start | bytes 1474564
  23.3 8.3 %copy-start.19 = (bf16[5,64,512]{2,1,0:T(8,128)(2,1)S(1)}, bf16[5,64,512]{2,1,0:T(8,128)(2,1)}, u32[]{:S(2)}) copy-start(bf16[5,64,512]{2,1,0:T(8,128)(2,1)} %q_ref.4) | copy-start | bytes 983044
  23.3 8.3 %copy-start.23 = (s32[8]{0:T(128)S(1)}, s32[8]{0:T(128)}, u32[]{:S(2)}) copy-start(s32[8]{0:T(128)} %band_ref.1) | copy-start | bytes 100
  23.3 65.5 %all-gather.3.cloned.1.call-start = ((), (), s32[]{:S(2)}) async-start(), calls=%async_computation.4 | async-start | bytes 1966080 | tf_op jit(solution)/shard_map/all_gather | solution.py:258
  25.3 6.3 %collective-permute-start = (bf16[2,5,16,512]{3,2,1,0:T(8,128)(2,1)S(1)}, bf16[2,5,16,512]{3,2,1,0:T(8,128)(2,1)S(1)}, u32[]{:S(2)}, u32[]{:S(2)}) collective-permute-start(bf16[2,5,16,512]{3,2,1,0:T(8,128)(2,1)S(1)} %pad_maximum_fusion.1), channel_id=1, source_target_pairs={{0,4},{4,8},{8,12},{12,16},{16,20},{20,24},{24,28},{28,32},{32,36}... | collective-permute-start | bytes 491528 | tf_op jit(solution)/shard_map/ppermute | solution.py:248
  31.6 4.7 %copy-start.21 = (bf16[2,5,16,512]{3,2,1,0:T(8,128)(2,1)}, bf16[2,5,16,512]{3,2,1,0:T(8,128)(2,1)S(1)}, u32[]{:S(2)}) copy-start(bf16[2,5,16,512]{3,2,1,0:T(8,128)(2,1)S(1)} %collective-permute-done.rim_ref) | copy-start | bytes 491524
  31.6 1.5 copy-start.24
  36.3 1.0 copy-start.1
  37.3 0.9 copy-start.25
  38.2 50.2 %copy-start.28 = (s32[20]{0:T(128)S(1)}, s32[20]{0:T(128)}, u32[]{:S(2)}) copy-start(s32[20]{0:T(128)} %param.20) | copy-start | bytes 244
  47.6 74.5 %all-to-all-start.2 = ((bf16[512,8,128]{2,1,0:T(8,128)(2,1)}), bf16[512,8,128]{2,1,0:T(8,128)(2,1)S(1)}, u32[]{:S(2)}, u32[]{:S(2)}) async-start(bf16[512,8,128]{2,1,0:T(8,128)(2,1)} %bitcast.16), calls=%async_computation.2 | async-start | bytes 2097152 | tf_op jit(solution)/shard_map/all_to_all | solution.py:284
  88.8 1.4 copy-start.17
  97.1 1.0 copy-start
  98.1 1.0 copy-start.2
  150.3 45.2 %all-to-all-start.3 = ((bf16[512,8,128]{2,1,0:T(8,128)(2,1)}), bf16[512,8,128]{2,1,0:T(8,128)(2,1)S(1)}, u32[]{:S(2)}, u32[]{:S(2)}) async-start(bf16[512,8,128]{2,1,0:T(8,128)(2,1)} %bitcast.15), calls=%async_computation.3 | async-start | bytes 2097152 | tf_op jit(solution)/shard_map/all_to_all | solution.py:315
  161.7 1.0 copy-start.5
  162.7 1.0 copy-start.14
  163.7 1.0 copy-start.16
  164.7 1.4 copy-start.18
  166.1 1.0 copy-start.20
  167.1 0.9 copy-start.22
  168.0 1.1 copy-start.26
  174.1 0.7 copy-start.6
  174.9 0.7 copy-start.8
  175.6 11.1 %collective-permute-start.1 = (f32[2,5,16,512]{3,2,1,0:T(8,128)}, f32[2,5,16,512]{3,2,1,0:T(8,128)}, u32[]{:S(2)}, u32[]{:S(2)}) collective-permute-start(f32[2,5,16,512]{3,2,1,0:T(8,128)} %get-tuple-element.27), channel_id=1, source_target_pairs={{4,0},{8,4},{12,8},{16,12},{20,16},{24,20},{28,24},{32,28},{36,32}... | collective-permute-start | bytes 983048 | tf_op jit(solution)/shard_map/ppermute | solution.py:333
  186.7 1.0 copy-start.7
  187.7 1.0 copy-start.9
Sparse Core Ops, SparseCore 0:
  26.3 59.0 all-gather.2
